TPU v7x, 32 devices: a whole 2x2x4 slice. The times are simulated.
32 devices in a mesh: groups: 2 (over x), seq: 16 (over z, y, core).
Axes of the slice: x: 2, y: 2, z: 4, core: 2. Of those that a mesh axis runs over, the one named last changes fastest.
Arguments:
- inputs: bfloat16 [16384, 768], P(('groups', 'seq')), parts along dimension 0, may hold values from -6 to 6
- gates: bfloat16 [16384, 768], P(('groups', 'seq')), parts along dimension 0, may hold values from -6 to 6
- cotangent: bfloat16 [16384, 768], P(('groups', 'seq')), parts along dimension 0, may hold values from -6 to 6
- first_factor: bfloat16 [16, 512, 512], P('seq'), may hold values from -0.25 to 0.25
- second_factor: bfloat16 [512, 16, 16], P('seq'), may hold values from -1.5 to 1.5
- channel_gain: float32 [768], replicated, may hold values from 0.1 to 1.9
Outputs:
- layer_output: bfloat16 [16384, 768], P(('groups', 'seq')), parts along dimension 0
- grad_inputs: bfloat16 [16384, 768], P(('groups', 'seq')), parts along dimension 0
- grad_gates: bfloat16 [16384, 768], P(('groups', 'seq')), parts along dimension 0
- grad_first: bfloat16 [32, 512, 512], P(('groups', 'seq')), parts along dimension 0
- grad_second: bfloat16 [1024, 16, 16], P(('groups', 'seq')), parts along dimension 0
- gain_grad: float32 [1536], P('groups'), parts along dimension 0
There are 2 independent parts, one for each index of `groups`. A program takes and returns all parts, laid end to end along the dimension named above; an argument that names none is the same for every part. Nothing has to cross between parts.
All inputs are finite; a program needn't handle non-finite values.
Results may differ from a plain program's by a relative error of at most 0.0085.
Values may be sent and summed in bfloat16 or wider, within the bound.
A program may use at most 64 MiB of HBM per device.

v0:
```python
import math
import jax
import jax.numpy as jnp
from jax import lax
from jax.sharding import PartitionSpec as P


def lower_mask(extent):
    row_ids = lax.broadcasted_iota(jnp.int32, (extent, extent), 0)
    col_ids = lax.broadcasted_iota(jnp.int32, (extent, extent), 1)
    return col_ids <= row_ids


def on_device(inputs, gates, cotangent, first_factor, second_factor, channel_gain):
    block_count = first_factor.shape[0]
    block_size = first_factor.shape[1]
    channels = inputs.shape[1]
    block_total = second_factor.shape[1]
    rows3 = inputs.reshape(block_count, block_size, channels)
    gates3 = gates.reshape(block_count, block_size, channels)
    upstream3 = cotangent.reshape(block_count, block_size, channels)
    mask_first = lower_mask(block_size)
    mask_second = lower_mask(block_total)
    first_masked = jnp.where(mask_first[None], first_factor, jnp.zeros((), first_factor.dtype))
    second_masked = jnp.where(mask_second[None], second_factor, jnp.zeros((), second_factor.dtype))
    norm_factor = 1.0 / math.sqrt(inputs.shape[0] * lax.axis_size("seq"))
    gates_cols, upstream_cols = (
        lax.all_to_all(gates3, "seq", split_axis=1, concat_axis=0, tiled=True),
        lax.all_to_all(upstream3, "seq", split_axis=1, concat_axis=0, tiled=True),
    )
    first_mixed = jnp.einsum(
        "kab,kbc->kac", first_masked, rows3, preferred_element_type=jnp.float32
    ).astype(jnp.bfloat16)
    columns = lax.all_to_all(first_mixed, "seq", split_axis=1, concat_axis=0, tiled=True)
    second_cols = jnp.einsum(
        "jab,bjc->ajc", second_masked, columns, preferred_element_type=jnp.float32
    ).astype(jnp.bfloat16)
    hidden_values = second_cols.astype(jnp.float32)
    gate_values = gates_cols.astype(jnp.float32)
    upstream_values = upstream_cols.astype(jnp.float32)
    output_cols = (gate_values * channel_gain * hidden_values).astype(jnp.bfloat16)
    hidden_cols = (upstream_values * gate_values * channel_gain).astype(jnp.bfloat16)
    grad_gate_cols = (upstream_values * channel_gain * hidden_values).astype(jnp.bfloat16)
    partial_gain = jnp.sum(upstream_values * gate_values * hidden_values, axis=(0, 1))
    grad_pairs = jnp.einsum(
        "ajc,bjc->jab", hidden_cols, columns, preferred_element_type=jnp.float32
    )
    grad_sec = jnp.where(mask_second[None], grad_pairs, jnp.zeros((), jnp.float32)).astype(
        jnp.bfloat16
    )
    back_cols = jnp.einsum(
        "jab,ajc->bjc", second_masked, hidden_cols, preferred_element_type=jnp.float32
    ).astype(jnp.bfloat16)
    back_rows, output_rows, grad_gate_rows = (
        lax.all_to_all(back_cols, "seq", split_axis=0, concat_axis=1, tiled=True),
        lax.all_to_all(output_cols, "seq", split_axis=0, concat_axis=1, tiled=True),
        lax.all_to_all(grad_gate_cols, "seq", split_axis=0, concat_axis=1, tiled=True),
    )
    gain_grad = lax.psum(partial_gain, "seq") * norm_factor
    grad_pairs_first = jnp.einsum(
        "kac,kbc->kab", back_rows, rows3, preferred_element_type=jnp.float32
    )
    grad_first = jnp.where(mask_first[None], grad_pairs_first, jnp.zeros((), jnp.float32)).astype(
        jnp.bfloat16
    )
    grad_in = jnp.einsum(
        "kab,kac->kbc", first_masked, back_rows, preferred_element_type=jnp.float32
    ).astype(jnp.bfloat16)
    token_rows = inputs.shape[0]
    return (
        output_rows.reshape(token_rows, channels),
        grad_in.reshape(token_rows, channels),
        grad_gate_rows.reshape(token_rows, channels),
        grad_first,
        grad_sec,
        gain_grad,
    )


def solution(mesh):
    placed = (
        P(("groups", "seq"), None),
        P(("groups", "seq"), None),
        P(("groups", "seq"), None),
        P("seq", None, None),
        P("seq", None, None),
        P(),
    )
    return jax.shard_map(
        on_device,
        mesh=mesh,
        in_specs=placed,
        out_specs=(
            P(("groups", "seq"), None),
            P(("groups", "seq"), None),
            P(("groups", "seq"), None),
            P(("groups", "seq"), None, None),
            P(("groups", "seq"), None, None),
            P("groups"),
        ),
        check_vma=False,
    )
```

profile of v0, /device:TPU:0, one launch (start us, length us, event | category | flops | bytes accessed | tf_op | source)
XLA Modules:
  0.0 196.3 jit_solution(10928412952804270693)
XLA Ops:
  0.6 1.1 copy-done
  1.8 1.6 fusion.5
  3.4 1.2 copy.83
  5.1 5.4 %reduce.2 = bf16[512,768]{1,0:T(8,128)(2,1)S(1)} reduce(bf16[512,1,768]{2,1,0:T(2,128)(2,1)S(1)} %bitcast.48, bf16[]{:T(256)} %broadcast.2), dimensions={1}, to_apply=%bitcast.46.reduce_sub_computation | reduce | bytes 1572866
  10.6 1.1 reshape.99
  11.6 7.6 %all-to-all-start.1 = ((bf16[16,2,12288]{2,1,0:T(2,128)(2,1)}), bf16[16,2,12288]{2,1,0:T(2,128)(2,1)}, u32[]{:S(2)}, u32[]{:S(2)}) async-start(bf16[16,2,12288]{2,1,0:T(2,128)(2,1)} %reshape.99), calls=%async_computation.1 | async-start | bytes 1572864 | tf_op jit(solution)/shard_map/all_to_all | solution.py:34
  19.2 1.2 copy.84
  20.4 5.4 %reduce = bf16[512,768]{1,0:T(8,128)(2,1)S(1)} reduce(bf16[512,1,768]{2,1,0:T(2,128)(2,1)S(1)} %bitcast.53, bf16[]{:T(256)} %broadcast.2), dimensions={1}, to_apply=%bitcast.47.reduce_sub_computation | reduce | bytes 1572866
  25.9 1.1 reshape.101
  26.9 11.0 %all-to-all-done.1 = bf16[16,2,12288]{2,1,0:T(2,128)(2,1)} async-done(((bf16[16,2,12288]{2,1,0:T(2,128)(2,1)}), bf16[16,2,12288]{2,1,0:T(2,128)(2,1)}, u32[]{:S(2)}, u32[]{:S(2)}) %all-to-all-start.1) | async-done | bytes 786464 | tf_op jit(solution)/shard_map/all_to_all | solution.py:34
  38.0 5.5 %all-to-all-start = ((bf16[16,2,12288]{2,1,0:T(2,128)(2,1)}), bf16[16,2,12288]{2,1,0:T(2,128)(2,1)}, u32[]{:S(2)}, u32[]{:S(2)}) async-start(bf16[16,2,12288]{2,1,0:T(2,128)(2,1)} %reshape.101), calls=%async_computation | async-start | bytes 1572864 | tf_op jit(solution)/shard_map/all_to_all | solution.py:28
  43.5 1.2 copy.82
  44.7 5.4 %reduce.1 = bf16[512,768]{1,0:T(8,128)(2,1)S(1)} reduce(bf16[512,1,768]{2,1,0:T(2,128)(2,1)S(1)} %bitcast.49, bf16[]{:T(256)} %broadcast.2), dimensions={1}, to_apply=%bitcast.45.reduce_sub_computation | reduce | bytes 1572866
  51.2 11.0 %all-to-all-done = bf16[16,2,12288]{2,1,0:T(2,128)(2,1)} async-done(((bf16[16,2,12288]{2,1,0:T(2,128)(2,1)}), bf16[16,2,12288]{2,1,0:T(2,128)(2,1)}, u32[]{:S(2)}, u32[]{:S(2)}) %all-to-all-start) | async-done | bytes 786464 | tf_op jit(solution)/shard_map/all_to_all | solution.py:28
  62.3 5.5 %all-to-all-start.3 = ((bf16[16,2,12288]{2,1,0:T(2,128)(2,1)}), bf16[16,2,12288]{2,1,0:T(2,128)(2,1)S(1)}, u32[]{:S(2)}, u32[]{:S(2)}) async-start(bf16[16,2,12288]{2,1,0:T(2,128)(2,1)} %reshape.103), calls=%async_computation.3 | async-start | bytes 1572864 | tf_op jit(solution)/shard_map/all_to_all | solution.py:29
  67.9 4.4 %reshape.100 = bf16[512,1,768]{2,1,0:T(2,128)(2,1)S(1)} reshape(bf16[16,2,12288]{2,1,0:T(2,128)(2,1)} %all-to-all-done.1) | data formatting | bytes 1572864
  73.3 4.4 %reshape.102 = bf16[512,1,768]{2,1,0:T(2,128)(2,1)S(1)} reshape(bf16[16,2,12288]{2,1,0:T(2,128)(2,1)} %all-to-all-done) | data formatting | bytes 1572864
  77.8 1.3 convert.3
  79.1 7.3 %all-to-all-done.3 = bf16[16,2,12288]{2,1,0:T(2,128)(2,1)S(1)} async-done(((bf16[16,2,12288]{2,1,0:T(2,128)(2,1)}), bf16[16,2,12288]{2,1,0:T(2,128)(2,1)S(1)}, u32[]{:S(2)}, u32[]{:S(2)}) %all-to-all-start.3) | async-done | bytes 786464 | tf_op jit(solution)/shard_map/all_to_all | solution.py:29
  88.9 2.4 %fusion.2 = (f32[768]{0:T(1024)S(1)}, bf16[16,32,768]{2,0,1:T(8,128)(2,1)S(1)}, bf16[16,32,768]{2,0,1:T(8,128)(2,1)S(1)}, bf16[16,32,768]{2,0,1:T(8,128)(2,1)S(1)}) fusion(f32[16,32,768]{2,1,0:T(8,128)S(1)} %copy-done.1, f32[16,32,768]{2,1,0:T(8,128)S(1)} %convert.4, f32[768]{0:T(1024)S(1)} %copy-done.7, bf16[16,32,768]{2,1,0:T(8,128)(2,1)S(1)} %bitcast.58, ...), kind=kOutput, calls=%fused_computation.5 | convolution fusion | flops 17702144 | bytes 6314240 | tf_op jit(solution)/shard_map/jab,bjc->ajc/dot_general | solution.py:35
  92.7 1.1 copy.54
  93.8 5.5 %all-to-all-start.4 = ((bf16[16,32,768]{2,1,0:T(8,128)(2,1)}), bf16[16,32,768]{2,1,0:T(8,128)(2,1)}, u32[]{:S(2)}, u32[]{:S(2)}) async-start(bf16[16,32,768]{2,1,0:T(8,128)(2,1)} %copy.54), calls=%async_computation.4 | async-start | bytes 1572864 | tf_op jit(solution)/shard_map/all_to_all | solution.py:55
  99.3 1.1 copy.56
  100.5 17.7 %all-to-all-done.4 = bf16[16,32,768]{2,1,0:T(8,128)(2,1)} async-done(((bf16[16,32,768]{2,1,0:T(8,128)(2,1)}), bf16[16,32,768]{2,1,0:T(8,128)(2,1)}, u32[]{:S(2)}, u32[]{:S(2)}) %all-to-all-start.4) | async-done | bytes 786464 | tf_op jit(solution)/shard_map/all_to_all | solution.py:55
  118.1 5.5 %all-to-all-start.5 = ((bf16[16,32,768]{2,1,0:T(8,128)(2,1)}), bf16[16,32,768]{2,1,0:T(8,128)(2,1)S(1)}, u32[]{:S(2)}, u32[]{:S(2)}) async-start(bf16[16,32,768]{2,1,0:T(8,128)(2,1)} %copy.56), calls=%async_computation.5 | async-start | bytes 1572864 | tf_op jit(solution)/shard_map/all_to_all | solution.py:57
  123.6 1.1 copy.48
  124.7 17.6 %all-to-all-done.5 = bf16[16,32,768]{2,1,0:T(8,128)(2,1)S(1)} async-done(((bf16[16,32,768]{2,1,0:T(8,128)(2,1)}), bf16[16,32,768]{2,1,0:T(8,128)(2,1)S(1)}, u32[]{:S(2)}, u32[]{:S(2)}) %all-to-all-start.5) | async-done | bytes 786464 | tf_op jit(solution)/shard_map/all_to_all | solution.py:57
  142.3 5.5 %all-to-all-start.2 = ((bf16[16,32,768]{2,1,0:T(8,128)(2,1)}), bf16[16,32,768]{2,1,0:T(8,128)(2,1)S(1)}, u32[]{:S(2)}, u32[]{:S(2)}) async-start(bf16[16,32,768]{2,1,0:T(8,128)(2,1)} %copy.48), calls=%async_computation.2 | async-start | bytes 1572864 | tf_op jit(solution)/shard_map/all_to_all | solution.py:56
  147.8 1.7 fusion.7
  150.3 38.5 %psum.7 = f32[768]{0:T(1024)S(1)} all-reduce(f32[768]{0:T(1024)S(1)} %get-tuple-element.30), channel_id=1, replica_groups=mesh['groups'=2,'seq'=16] {'seq'}, use_global_device_ids=true, to_apply=%region_1.2 | all-reduce | flops 768 | bytes 6144 | tf_op jit(solution)/shard_map/psum | solution.py:59
  189.4 2.5 %fusion.6 = bf16[1,512,512]{2,1,0:T(8,128)(2,1)} fusion(bf16[512,768]{1,0:T(8,128)(2,1)} %bitcast.10, bf16[512,768]{1,0:T(8,128)(2,1)S(1)} %copy-done), kind=kOutput, calls=%fused_computation.16 | convolution fusion | flops 403439616 | bytes 2097152 | tf_op jit(solution)/shard_map/kac,kbc->kab/dot_general | solution.py:60
  191.9 2.6 %convolution_convert_fusion = bf16[512,768]{1,0:T(8,128)(2,1)} fusion(bf16[512,768]{1,0:T(8,128)(2,1)} %bitcast.10, bf16[1,512,512]{2,1,0:T(8,128)(2,1)S(1)} %copy-done.8), kind=kOutput, calls=%fused_computation.8 | convolution fusion | flops 403570688 | bytes 2097152 | tf_op jit(solution)/shard_map/kab,kac->kbc/dot_general | solution.py:66
  (32 shorter events, 9.8 us)
Async XLA Ops:
  0.6 1.1 copy-start
  11.6 7.6 %copy-start.4 = (bf16[512,768]{1,0:T(8,128)(2,1)S(1)}, bf16[512,768]{1,0:T(8,128)(2,1)}, u32[]{:S(2)}) copy-start(bf16[512,768]{1,0:T(8,128)(2,1)} %param.7) | copy-start | bytes 2359300
  11.6 26.3 %all-to-all-start.1 = ((bf16[16,2,12288]{2,1,0:T(2,128)(2,1)}), bf16[16,2,12288]{2,1,0:T(2,128)(2,1)}, u32[]{:S(2)}, u32[]{:S(2)}) async-start(bf16[16,2,12288]{2,1,0:T(2,128)(2,1)} %reshape.99), calls=%async_computation.1 | async-start | bytes 1572864 | tf_op jit(solution)/shard_map/all_to_all | solution.py:34
  26.9 16.6 %copy-start.5 = (bf16[512,768]{1,0:T(8,128)(2,1)S(1)}, bf16[512,768]{1,0:T(8,128)(2,1)}, u32[]{:S(2)}) copy-start(bf16[512,768]{1,0:T(8,128)(2,1)} %param.8) | copy-start | bytes 2359300
  38.0 24.3 %all-to-all-start = ((bf16[16,2,12288]{2,1,0:T(2,128)(2,1)}), bf16[16,2,12288]{2,1,0:T(2,128)(2,1)}, u32[]{:S(2)}, u32[]{:S(2)}) async-start(bf16[16,2,12288]{2,1,0:T(2,128)(2,1)} %reshape.101), calls=%async_computation | async-start | bytes 1572864 | tf_op jit(solution)/shard_map/all_to_all | solution.py:28
  50.2 17.6 %copy-start.6 = (bf16[32,16,16]{0,2,1:T(8,128)(2,1)S(1)}, bf16[32,16,16]{0,2,1:T(8,128)(2,1)}, u32[]{:S(2)}) copy-start(bf16[32,16,16]{0,2,1:T(8,128)(2,1)} %param.10) | copy-start | bytes 49156
  62.3 24.2 %all-to-all-start.3 = ((bf16[16,2,12288]{2,1,0:T(2,128)(2,1)}), bf16[16,2,12288]{2,1,0:T(2,128)(2,1)S(1)}, u32[]{:S(2)}, u32[]{:S(2)}) async-start(bf16[16,2,12288]{2,1,0:T(2,128)(2,1)} %reshape.103), calls=%async_computation.3 | async-start | bytes 1572864 | tf_op jit(solution)/shard_map/all_to_all | solution.py:29
  87.2 0.7 copy-start.7
  87.3 1.4 copy-start.1
  87.3 1.6 copy-start.2
  91.4 0.9 copy-start.3
  93.8 24.3 %all-to-all-start.4 = ((bf16[16,32,768]{2,1,0:T(8,128)(2,1)}), bf16[16,32,768]{2,1,0:T(8,128)(2,1)}, u32[]{:S(2)}, u32[]{:S(2)}) async-start(bf16[16,32,768]{2,1,0:T(8,128)(2,1)} %copy.54), calls=%async_computation.4 | async-start | bytes 1572864 | tf_op jit(solution)/shard_map/all_to_all | solution.py:55
  118.1 24.2 %all-to-all-start.5 = ((bf16[16,32,768]{2,1,0:T(8,128)(2,1)}), bf16[16,32,768]{2,1,0:T(8,128)(2,1)S(1)}, u32[]{:S(2)}, u32[]{:S(2)}) async-start(bf16[16,32,768]{2,1,0:T(8,128)(2,1)} %copy.56), calls=%async_computation.5 | async-start | bytes 1572864 | tf_op jit(solution)/shard_map/all_to_all | solution.py:57
  142.3 52.2 %all-to-all-start.2 = ((bf16[16,32,768]{2,1,0:T(8,128)(2,1)}), bf16[16,32,768]{2,1,0:T(8,128)(2,1)S(1)}, u32[]{:S(2)}, u32[]{:S(2)}) async-start(bf16[16,32,768]{2,1,0:T(8,128)(2,1)} %copy.48), calls=%async_computation.2 | async-start | bytes 1572864 | tf_op jit(solution)/shard_map/all_to_all | solution.py:56
  149.5 42.4 %copy-start.8 = (bf16[1,512,512]{2,1,0:T(8,128)(2,1)S(1)}, bf16[1,512,512]{2,1,0:T(8,128)(2,1)}, u32[]{:S(2)}) copy-start(bf16[1,512,512]{2,1,0:T(8,128)(2,1)} %param.9) | copy-start | bytes 1572868
where the time goes:
time: 197 us; the launch traced here: 196 us
  waiting for transfers between devices  64.6 us (33%)
  blocking collectives  38.5 us (20%)
  starting transfers between devices  35.1 us (18%)
  local copies, waits for them, and re-layouts  27.5 us (14%)
  other arithmetic  18.3 us (9%)
  matrix products  11.3 us (6%)
    psum x1, blocking collectives, on_device(): gain_grad = lax.psum(partial_gain, 'seq') * norm_factor  38.5 us
    unnamed x30, local copies, waits for them, and re-layouts  20.3 us
    all_to_all x1, waiting for transfers between devices, on_device(): lax.all_to_all(back_cols, 'seq', split_axis=0, concat_axis=1, tiled=True)  17.7 us
    all_to_all x1, waiting for transfers between devices, on_device(): lax.all_to_all(grad_gate_cols, 'seq', split_axis=0, concat_axis=1, tiled=...  17.6 us
    unnamed x3, other arithmetic  16.3 us
    all_to_all x1, waiting for transfers between devices, on_device(): lax.all_to_all(first_mixed, 'seq', split_axis=1, concat_axis=0, tiled=True)  11 us
    all_to_all x1, waiting for transfers between devices, on_device(): lax.all_to_all(gates3, 'seq', split_axis=1, concat_axis=0, tiled=True)  11 us
    all_to_all x1, starting transfers between devices, on_device(): lax.all_to_all(first_mixed, 'seq', split_axis=1, concat_axis=0, tiled=True)  7.57 us
  transfers between devices with their start and end apart: 6, of which 5 were waited for; matrix products, arithmetic and copies ran while one was open for 19% of the time, Pallas kernels for 0%

commit v1 on v0

--- a/solution.py
+++ b/solution.py
@@ -3,6 +3,29 @@
 import jax.numpy as jnp
 from jax import lax
 from jax.sharding import PartitionSpec as P
+
+
+def cut_along(x, dim, devices):
+    shape = x.shape
+    blocks = x.reshape(*shape[:dim], devices, shape[dim] // devices, *shape[dim + 1 :])
+    return jnp.moveaxis(blocks, dim, 0)
+
+
+def in_order(pieces, dim):
+    shape = list(pieces.shape[1:])
+    shape[dim] *= pieces.shape[0]
+    return jnp.moveaxis(pieces, 0, dim).reshape(shape)
+
+
+def pairwise_exchange(value, axis, split_dim, concat_dim):
+    size, index = (lax.axis_size(axis), lax.axis_index(axis))
+    blocks = cut_along(value, split_dim, size)
+    finished = [blocks[index]]
+    for step in range(1, size):
+        sent = blocks[index ^ step]
+        finished.append(lax.ppermute(sent, axis, [(i, i ^ step) for i in range(size)]))
+    blocks = jnp.stack(finished)[index ^ jnp.arange(size)]
+    return in_order(blocks, concat_dim)
 
 
 def lower_mask(extent):
@@ -26,7 +49,7 @@
     norm_factor = 1.0 / math.sqrt(inputs.shape[0] * lax.axis_size("seq"))
     gates_cols, upstream_cols = (
         lax.all_to_all(gates3, "seq", split_axis=1, concat_axis=0, tiled=True),
-        lax.all_to_all(upstream3, "seq", split_axis=1, concat_axis=0, tiled=True),
+        pairwise_exchange(upstream3, "seq", 1, 0),
     )
     first_mixed = jnp.einsum(
         "kab,kbc->kac", first_masked, rows3, preferred_element_type=jnp.float32

time: 197 us -> 220 us (1.12)
  waiting for transfers between devices: 64.6 us -> 82.9 us
  starting transfers between devices: 35.1 us -> 47.1 us
  other arithmetic: 18.3 us -> 11.6 us
    ppermute x0 -> x15, waiting for transfers between devices: none -> 47.8 us  [pairwise_exchange(): lax.ppermute(sent, axis, [(i, i ^ step) for i in range(size)])]
    ppermute x0 -> x15, starting transfers between devices: none -> 20.7 us  [pairwise_exchange(): lax.ppermute(sent, axis, [(i, i ^ step) for i in range(size)])]
    all_to_all x1, waiting for transfers between devices: 17.6 us -> 0.01 us  [on_device(): lax.all_to_all(grad_gate_cols, 'seq', split_axis=0, concat_axis=1, tiled=...]
    all_to_all x1, waiting for transfers between devices: 0.01 us -> 17.6 us  [on_device(): lax.all_to_all(output_cols, 'seq', split_axis=0, concat_axis=1, tiled=True)]
    all_to_all x1, waiting for transfers between devices: 11 us -> 0.01 us  [on_device(): lax.all_to_all(first_mixed, 'seq', split_axis=1, concat_axis=0, tiled=True)]
    all_to_all x1, waiting for transfers between devices: 11 us -> 0.01 us  [on_device(): lax.all_to_all(gates3, 'seq', split_axis=1, concat_axis=0, tiled=True)]
    all_to_all x1 -> x0, waiting for transfers between devices: 7.34 us -> none  [on_device(): lax.all_to_all(upstream3, 'seq', split_axis=1, concat_axis=0, tiled=True)]
    all_to_all x1 -> x0, starting transfers between devices: 5.48 us -> none  [on_device(): lax.all_to_all(upstream3, 'seq', split_axis=1, concat_axis=0, tiled=True)]
  transfers between devices with their start and end apart: 6 -> 20, of which waited for: 5 -> 12; matrix products, arithmetic and copies ran while one was open for 19% -> 13% of each run, Pallas kernels for 0% -> 0%
where the time goes in v1:
time: 220 us; the launch traced here: 219 us
  waiting for transfers between devices  82.9 us (38%)
  starting transfers between devices  47.1 us (21%)
  blocking collectives  38.2 us (17%)
  local copies, waits for them, and re-layouts  26.2 us (12%)
  other arithmetic  11.6 us (5%)
  matrix products  11.5 us (5%)
    ppermute x15, waiting for transfers between devices, pairwise_exchange(): lax.ppermute(sent, axis, [(i, i ^ step) for i in range(size)])  47.8 us
    psum x1, blocking collectives, on_device(): gain_grad = lax.psum(partial_gain, 'seq') * norm_factor  38.2 us
    ppermute x15, starting transfers between devices, pairwise_exchange(): lax.ppermute(sent, axis, [(i, i ^ step) for i in range(size)])  20.7 us
    all_to_all x1, waiting for transfers between devices, on_device(): lax.all_to_all(output_cols, 'seq', split_axis=0, concat_axis=1, tiled=True)  17.6 us
    all_to_all x1, waiting for transfers between devices, on_device(): lax.all_to_all(back_cols, 'seq', split_axis=0, concat_axis=1, tiled=True)  17.5 us
    unnamed x62, local copies, waits for them, and re-layouts  17.1 us
    unnamed x2, other arithmetic  10.9 us
    all_to_all x1, starting transfers between devices, on_device(): lax.all_to_all(first_mixed, 'seq', split_axis=1, concat_axis=0, tiled=True)  7.57 us
  transfers between devices with their start and end apart: 20, of which 12 were waited for; matrix products, arithmetic and copies ran while one was open for 13% of the time, Pallas kernels for 0%

profile of v1, /device:TPU:0, one launch (start us, length us, event | category | flops | bytes accessed | tf_op | source)
XLA Modules:
  0.0 218.6 jit_solution(8174384369541128060)
XLA Ops:
  1.8 1.6 fusion.6
  5.1 5.4 %reduce.1 = bf16[512,768]{1,0:T(8,128)(2,1)S(1)} reduce(bf16[512,1,768]{2,1,0:T(2,128)(2,1)S(1)} %bitcast.103, bf16[]{:T(256)} %broadcast.37), dimensions={1}, to_apply=%bitcast.101.reduce_sub_computation | reduce | bytes 1572866
  11.6 7.6 %all-to-all-start.1 = ((bf16[16,2,12288]{2,1,0:T(2,128)(2,1)}), bf16[16,2,12288]{2,1,0:T(2,128)(2,1)}, u32[]{:S(2)}, u32[]{:S(2)}) async-start(bf16[16,2,12288]{2,1,0:T(2,128)(2,1)} %reshape.121), calls=%async_computation.1 | async-start | bytes 1572864 | tf_op jit(solution)/shard_map/all_to_all | solution.py:57
  20.1 4.2 %collective-permute-start.14 = (bf16[1,32,768]{2,1,0:T(8,128)(2,1)S(1)}, bf16[1,32,768]{2,1,0:T(8,128)(2,1)}, u32[]{:S(2)}, u32[]{:S(2)}) collective-permute-start(bf16[1,32,768]{2,1,0:T(8,128)(2,1)S(1)} %get-tuple-element.34), channel_id=1, source_target_pairs={{0,15},{1,14},{2,13},{3,12},{4,11},{5,10},{6,9},{7,8},{8,7},{9,6},... | collective-permute-start | bytes 147464 | tf_op jit(solution)/shard_map/ppermute | solution.py:26
  24.7 3.2 %collective-permute-start.12 = (bf16[1,32,768]{2,1,0:T(8,128)(2,1)S(1)}, bf16[1,32,768]{2,1,0:T(8,128)(2,1)}, u32[]{:S(2)}, u32[]{:S(2)}) collective-permute-start(bf16[1,32,768]{2,1,0:T(8,128)(2,1)S(1)} %get-tuple-element.36), channel_id=1, source_target_pairs={{0,13},{1,12},{2,15},{3,14},{4,9},{5,8},{6,11},{7,10},{8,5},{9,4},... | collective-permute-start | bytes 147464 | tf_op jit(solution)/shard_map/ppermute | solution.py:26
  29.9 5.4 %reduce = bf16[512,768]{1,0:T(8,128)(2,1)S(1)} reduce(bf16[512,1,768]{2,1,0:T(2,128)(2,1)S(1)} %bitcast.104, bf16[]{:T(256)} %broadcast.37), dimensions={1}, to_apply=%bitcast.102.reduce_sub_computation | reduce | bytes 1572866
  36.5 1.7 collective-permute-start.1
  38.9 2.1 collective-permute-done.1
  41.4 3.5 %collective-permute-done.2 = bf16[1,32,768]{2,1,0:T(8,128)(2,1)S(1)} collective-permute-done((bf16[1,32,768]{2,1,0:T(8,128)(2,1)S(1)}, bf16[1,32,768]{2,1,0:T(8,128)(2,1)S(1)}, u32[]{:S(2)}, u32[]{:S(2)}) %collective-permute-start.2) | collective-permute-done | bytes 49184 | tf_op jit(solution)/shard_map/ppermute | solution.py:26
  45.0 4.1 %collective-permute-done.3 = bf16[1,32,768]{2,1,0:T(8,128)(2,1)S(1)} collective-permute-done((bf16[1,32,768]{2,1,0:T(8,128)(2,1)S(1)}, bf16[1,32,768]{2,1,0:T(8,128)(2,1)S(1)}, u32[]{:S(2)}, u32[]{:S(2)}) %collective-permute-start.3) | collective-permute-done | bytes 49184 | tf_op jit(solution)/shard_map/ppermute | solution.py:26
  49.1 3.5 %collective-permute-done.4 = bf16[1,32,768]{2,1,0:T(8,128)(2,1)S(1)} collective-permute-done((bf16[1,32,768]{2,1,0:T(8,128)(2,1)S(1)}, bf16[1,32,768]{2,1,0:T(8,128)(2,1)S(1)}, u32[]{:S(2)}, u32[]{:S(2)}) %collective-permute-start.4) | collective-permute-done | bytes 49184 | tf_op jit(solution)/shard_map/ppermute | solution.py:26
  53.1 4.4 %collective-permute-done.5 = bf16[1,32,768]{2,1,0:T(8,128)(2,1)S(1)} collective-permute-done((bf16[1,32,768]{2,1,0:T(8,128)(2,1)S(1)}, bf16[1,32,768]{2,1,0:T(8,128)(2,1)S(1)}, u32[]{:S(2)}, u32[]{:S(2)}) %collective-permute-start.5) | collective-permute-done | bytes 49184 | tf_op jit(solution)/shard_map/ppermute | solution.py:26
  57.6 4.4 %collective-permute-done.6 = bf16[1,32,768]{2,1,0:T(8,128)(2,1)S(1)} collective-permute-done((bf16[1,32,768]{2,1,0:T(8,128)(2,1)S(1)}, bf16[1,32,768]{2,1,0:T(8,128)(2,1)S(1)}, u32[]{:S(2)}, u32[]{:S(2)}) %collective-permute-start.6) | collective-permute-done | bytes 49184 | tf_op jit(solution)/shard_map/ppermute | solution.py:26
  62.0 2.7 %collective-permute-start.7 = (bf16[1,32,768]{2,1,0:T(8,128)(2,1)S(1)}, bf16[1,32,768]{2,1,0:T(8,128)(2,1)S(1)}, u32[]{:S(2)}, u32[]{:S(2)}) collective-permute-start(bf16[1,32,768]{2,1,0:T(8,128)(2,1)S(1)} %copy-done.10), channel_id=1, source_target_pairs={{0,8},{1,9},{2,10},{3,11},{4,12},{5,13},{6,14},{7,15},{8,0},{9,1},... | collective-permute-start | bytes 147464 | tf_op jit(solution)/shard_map/ppermute | solution.py:26
  64.7 2.2 %collective-permute-done.7 = bf16[1,32,768]{2,1,0:T(8,128)(2,1)S(1)} collective-permute-done((bf16[1,32,768]{2,1,0:T(8,128)(2,1)S(1)}, bf16[1,32,768]{2,1,0:T(8,128)(2,1)S(1)}, u32[]{:S(2)}, u32[]{:S(2)}) %collective-permute-start.7) | collective-permute-done | bytes 49184 | tf_op jit(solution)/shard_map/ppermute | solution.py:26
  68.2 3.3 %collective-permute-done.8 = bf16[1,32,768]{2,1,0:T(8,128)(2,1)S(1)} collective-permute-done((bf16[1,32,768]{2,1,0:T(8,128)(2,1)S(1)}, bf16[1,32,768]{2,1,0:T(8,128)(2,1)S(1)}, u32[]{:S(2)}, u32[]{:S(2)}) %collective-permute-start.8) | collective-permute-done | bytes 49184 | tf_op jit(solution)/shard_map/ppermute | solution.py:26
  71.6 2.6 %collective-permute-start.9 = (bf16[1,32,768]{2,1,0:T(8,128)(2,1)S(1)}, bf16[1,32,768]{2,1,0:T(8,128)(2,1)S(1)}, u32[]{:S(2)}, u32[]{:S(2)}) collective-permute-start(bf16[1,32,768]{2,1,0:T(8,128)(2,1)S(1)} %copy-done.8), channel_id=1, source_target_pairs={{0,10},{1,11},{2,8},{3,9},{4,14},{5,15},{6,12},{7,13},{8,2},{9,3},... | collective-permute-start | bytes 147464 | tf_op jit(solution)/shard_map/ppermute | solution.py:26
  74.2 4.3 %all-to-all-start = ((bf16[16,2,12288]{2,1,0:T(2,128)(2,1)}), bf16[16,2,12288]{2,1,0:T(2,128)(2,1)S(1)}, u32[]{:S(2)}, u32[]{:S(2)}) async-start(bf16[16,2,12288]{2,1,0:T(2,128)(2,1)} %reshape.123), calls=%async_computation | async-start | bytes 1572864 | tf_op jit(solution)/shard_map/all_to_all | solution.py:51
  78.8 3.3 %collective-permute-start.10 = (bf16[1,32,768]{2,1,0:T(8,128)(2,1)S(1)}, bf16[1,32,768]{2,1,0:T(8,128)(2,1)S(1)}, u32[]{:S(2)}, u32[]{:S(2)}) collective-permute-start(bf16[1,32,768]{2,1,0:T(8,128)(2,1)S(1)} %get-tuple-element.38), channel_id=1, source_target_pairs={{0,11},{1,10},{2,9},{3,8},{4,15},{5,14},{6,13},{7,12},{8,3},{9,2},... | collective-permute-start | bytes 147464 | tf_op jit(solution)/shard_map/ppermute | solution.py:26
  82.0 19.9 %collective-permute-done.10 = bf16[1,32,768]{2,1,0:T(8,128)(2,1)S(1)} collective-permute-done((bf16[1,32,768]{2,1,0:T(8,128)(2,1)S(1)}, bf16[1,32,768]{2,1,0:T(8,128)(2,1)S(1)}, u32[]{:S(2)}, u32[]{:S(2)}) %collective-permute-start.10) | collective-permute-done | bytes 49184 | tf_op jit(solution)/shard_map/ppermute | solution.py:26
  105.1 1.5 gather_fusion
  106.6 4.4 %reshape.122 = bf16[512,1,768]{2,1,0:T(2,128)(2,1)S(1)} reshape(bf16[16,2,12288]{2,1,0:T(2,128)(2,1)} %all-to-all-done.1) | data formatting | bytes 1572864
  114.2 3.5 %fusion.3 = (f32[768]{0:T(1024)S(1)}, bf16[16,32,768]{2,0,1:T(8,128)(2,1)}, bf16[16,32,768]{2,0,1:T(8,128)(2,1)}, bf16[16,32,768]{2,0,1:T(8,128)(2,1)S(1)}) fusion(f32[16,32,768]{2,1,0:T(8,128)S(1)} %convert.3, bf16[16,32,768]{2,1,0:T(8,128)(2,1)S(1)} %copy-done.3, f32[768]{0:T(1024)S(1)} %copy-done.18, bf16[16,32,768]{2,1,0:T(8,128)(2,1)S(1)} %bitcast.116, ...), kind=kOutput, calls=%fused_computation.8 | convolution fusion | flops 18095360 | bytes 5527808 | tf_op jit(solution)/shard_map/jab,bjc->ajc/dot_general | solution.py:58
  117.7 1.5 fusion.5
  120.4 3.6 %all-to-all-start.3 = ((bf16[16,32,768]{2,1,0:T(8,128)(2,1)}), bf16[16,32,768]{2,1,0:T(8,128)(2,1)S(1)}, u32[]{:S(2)}, u32[]{:S(2)}) async-start(bf16[16,32,768]{2,1,0:T(8,128)(2,1)} %copy.49), calls=%async_computation.3 | async-start | bytes 1572864 | tf_op jit(solution)/shard_map/all_to_all | solution.py:78
  125.1 17.5 %all-to-all-done.3 = bf16[16,32,768]{2,1,0:T(8,128)(2,1)S(1)} async-done(((bf16[16,32,768]{2,1,0:T(8,128)(2,1)}), bf16[16,32,768]{2,1,0:T(8,128)(2,1)S(1)}, u32[]{:S(2)}, u32[]{:S(2)}) %all-to-all-start.3) | async-done | bytes 786464 | tf_op jit(solution)/shard_map/all_to_all | solution.py:78
  142.7 5.4 %all-to-all-start.2 = ((bf16[16,32,768]{2,1,0:T(8,128)(2,1)}), bf16[16,32,768]{2,1,0:T(8,128)(2,1)S(1)}, u32[]{:S(2)}, u32[]{:S(2)}) async-start(bf16[16,32,768]{2,1,0:T(8,128)(2,1)} %copy.45), calls=%async_computation.2 | async-start | bytes 1572864 | tf_op jit(solution)/shard_map/all_to_all | solution.py:79
  149.3 17.6 %all-to-all-done.2 = bf16[16,32,768]{2,1,0:T(8,128)(2,1)S(1)} async-done(((bf16[16,32,768]{2,1,0:T(8,128)(2,1)}), bf16[16,32,768]{2,1,0:T(8,128)(2,1)S(1)}, u32[]{:S(2)}, u32[]{:S(2)}) %all-to-all-start.2) | async-done | bytes 786464 | tf_op jit(solution)/shard_map/all_to_all | solution.py:79
  166.8 5.5 %all-to-all-start.4 = ((bf16[16,32,768]{2,1,0:T(8,128)(2,1)}), bf16[16,32,768]{2,1,0:T(8,128)(2,1)S(1)}, u32[]{:S(2)}, u32[]{:S(2)}) async-start(bf16[16,32,768]{2,1,0:T(8,128)(2,1)} %copy.50), calls=%async_computation.4 | async-start | bytes 1572864 | tf_op jit(solution)/shard_map/all_to_all | solution.py:80
  172.3 2.0 fusion.8
  175.1 38.2 %psum.7 = f32[768]{0:T(1024)S(1)} all-reduce(f32[768]{0:T(1024)S(1)} %get-tuple-element.30), channel_id=1, replica_groups=mesh['groups'=2,'seq'=16] {'seq'}, use_global_device_ids=true, to_apply=%region_1.2 | all-reduce | flops 768 | bytes 6144 | tf_op jit(solution)/shard_map/psum | solution.py:82
  215.3 1.5 convolution_convert_fusion
  (93 shorter events, 25.9 us)
Async XLA Ops:
  10.6 8.7 %copy-start.2 = (bf16[512,768]{1,0:T(8,128)(2,1)S(1)}, bf16[512,768]{1,0:T(8,128)(2,1)}, u32[]{:S(2)}) copy-start(bf16[512,768]{1,0:T(8,128)(2,1)} %param.8) | copy-start | bytes 2359300
  11.6 16.8 %copy-start.7 = (bf16[32,16,16]{0,2,1:T(8,128)(2,1)S(1)}, bf16[32,16,16]{0,2,1:T(8,128)(2,1)}, u32[]{:S(2)}) copy-start(bf16[32,16,16]{0,2,1:T(8,128)(2,1)} %param.10) | copy-start | bytes 49156
  11.6 17.0 %copy-start.5 = (bf16[512,768]{1,0:T(8,128)(2,1)S(1)}, bf16[512,768]{1,0:T(8,128)(2,1)}, u32[]{:S(2)}) copy-start(bf16[512,768]{1,0:T(8,128)(2,1)} %param.7) | copy-start | bytes 2359300
  11.6 62.5 %all-to-all-start.1 = ((bf16[16,2,12288]{2,1,0:T(2,128)(2,1)}), bf16[16,2,12288]{2,1,0:T(2,128)(2,1)}, u32[]{:S(2)}, u32[]{:S(2)}) async-start(bf16[16,2,12288]{2,1,0:T(2,128)(2,1)} %reshape.121), calls=%async_computation.1 | async-start | bytes 1572864 | tf_op jit(solution)/shard_map/all_to_all | solution.py:57
  20.1 84.2 %collective-permute-start.14 = (bf16[1,32,768]{2,1,0:T(8,128)(2,1)S(1)}, bf16[1,32,768]{2,1,0:T(8,128)(2,1)}, u32[]{:S(2)}, u32[]{:S(2)}) collective-permute-start(bf16[1,32,768]{2,1,0:T(8,128)(2,1)S(1)} %get-tuple-element.34), channel_id=1, source_target_pairs={{0,15},{1,14},{2,13},{3,12},{4,11},{5,10},{6,9},{7,8},{8,7},{9,6},... | collective-permute-start | bytes 147464 | tf_op jit(solution)/shard_map/ppermute | solution.py:26
  24.4 79.1 %collective-permute-start.13 = (bf16[1,32,768]{2,1,0:T(8,128)(2,1)S(1)}, bf16[1,32,768]{2,1,0:T(8,128)(2,1)}, u32[]{:S(2)}, u32[]{:S(2)}) collective-permute-start(bf16[1,32,768]{2,1,0:T(8,128)(2,1)S(1)} %get-tuple-element.35), channel_id=1, source_target_pairs={{0,14},{1,15},{2,12},{3,13},{4,10},{5,11},{6,8},{7,9},{8,6},{9,7},... | collective-permute-start | bytes 147464 | tf_op jit(solution)/shard_map/ppermute | solution.py:26
  24.7 78.0 %collective-permute-start.12 = (bf16[1,32,768]{2,1,0:T(8,128)(2,1)S(1)}, bf16[1,32,768]{2,1,0:T(8,128)(2,1)}, u32[]{:S(2)}, u32[]{:S(2)}) collective-permute-start(bf16[1,32,768]{2,1,0:T(8,128)(2,1)S(1)} %get-tuple-element.36), channel_id=1, source_target_pairs={{0,13},{1,12},{2,15},{3,14},{4,9},{5,8},{6,11},{7,10},{8,5},{9,4},... | collective-permute-start | bytes 147464 | tf_op jit(solution)/shard_map/ppermute | solution.py:26
  27.9 74.0 %collective-permute-start.11 = (bf16[1,32,768]{2,1,0:T(8,128)(2,1)S(1)}, bf16[1,32,768]{2,1,0:T(8,128)(2,1)}, u32[]{:S(2)}, u32[]{:S(2)}) collective-permute-start(bf16[1,32,768]{2,1,0:T(8,128)(2,1)S(1)} %get-tuple-element.37), channel_id=1, source_target_pairs={{0,12},{1,13},{2,14},{3,15},{4,8},{5,9},{6,10},{7,11},{8,4},{9,5},... | collective-permute-start | bytes 147464 | tf_op jit(solution)/shard_map/ppermute | solution.py:26
  28.3 8.2 %collective-permute-start = (bf16[1,32,768]{2,1,0:T(8,128)(2,1)}, bf16[1,32,768]{2,1,0:T(8,128)(2,1)}, u32[]{:S(2)}, u32[]{:S(2)}) collective-permute-start(bf16[1,32,768]{2,1,0:T(8,128)(2,1)} %get-tuple-element.48), channel_id=1, source_target_pairs={{0,1},{1,0},{2,3},{3,2},{4,5},{5,4},{6,7},{7,6},{8,9},{9,8},{10,11... | collective-permute-start | bytes 147464 | tf_op jit(solution)/shard_map/ppermute | solution.py:26
  35.3 5.7 %copy-start.15 = (bf16[1,32,768]{2,1,0:T(8,128)(2,1)S(1)}, bf16[1,32,768]{2,1,0:T(8,128)(2,1)}, u32[]{:S(2)}) copy-start(bf16[1,32,768]{2,1,0:T(8,128)(2,1)} %get-tuple-element.46) | copy-start | bytes 147460
  35.3 9.6 %copy-start.14 = (bf16[1,32,768]{2,1,0:T(8,128)(2,1)S(1)}, bf16[1,32,768]{2,1,0:T(8,128)(2,1)}, u32[]{:S(2)}) copy-start(bf16[1,32,768]{2,1,0:T(8,128)(2,1)} %get-tuple-element.45) | copy-start | bytes 147460
  35.3 13.7 %copy-start.13 = (bf16[1,32,768]{2,1,0:T(8,128)(2,1)S(1)}, bf16[1,32,768]{2,1,0:T(8,128)(2,1)}, u32[]{:S(2)}) copy-start(bf16[1,32,768]{2,1,0:T(8,128)(2,1)} %get-tuple-element.44) | copy-start | bytes 147460
  35.3 17.2 %copy-start.12 = (bf16[1,32,768]{2,1,0:T(8,128)(2,1)S(1)}, bf16[1,32,768]{2,1,0:T(8,128)(2,1)}, u32[]{:S(2)}) copy-start(bf16[1,32,768]{2,1,0:T(8,128)(2,1)} %get-tuple-element.43) | copy-start | bytes 147460
  35.4 22.2 %copy-start.11 = (bf16[1,32,768]{2,1,0:T(8,128)(2,1)S(1)}, bf16[1,32,768]{2,1,0:T(8,128)(2,1)}, u32[]{:S(2)}) copy-start(bf16[1,32,768]{2,1,0:T(8,128)(2,1)} %get-tuple-element.42) | copy-start | bytes 147460
  35.4 26.6 %copy-start.10 = (bf16[1,32,768]{2,1,0:T(8,128)(2,1)S(1)}, bf16[1,32,768]{2,1,0:T(8,128)(2,1)}, u32[]{:S(2)}) copy-start(bf16[1,32,768]{2,1,0:T(8,128)(2,1)} %get-tuple-element.41) | copy-start | bytes 147460
  35.4 31.6 %copy-start.9 = (bf16[1,32,768]{2,1,0:T(8,128)(2,1)S(1)}, bf16[1,32,768]{2,1,0:T(8,128)(2,1)}, u32[]{:S(2)}) copy-start(bf16[1,32,768]{2,1,0:T(8,128)(2,1)} %get-tuple-element.40) | copy-start | bytes 147460
  35.4 36.2 %copy-start.8 = (bf16[1,32,768]{2,1,0:T(8,128)(2,1)S(1)}, bf16[1,32,768]{2,1,0:T(8,128)(2,1)}, u32[]{:S(2)}) copy-start(bf16[1,32,768]{2,1,0:T(8,128)(2,1)} %get-tuple-element.39) | copy-start | bytes 147460
  36.5 4.6 %collective-permute-start.1 = (bf16[1,32,768]{2,1,0:T(8,128)(2,1)S(1)}, bf16[1,32,768]{2,1,0:T(8,128)(2,1)S(1)}, u32[]{:S(2)}, u32[]{:S(2)}) collective-permute-start(bf16[1,32,768]{2,1,0:T(8,128)(2,1)S(1)} %copy-done.16), channel_id=1, source_target_pairs={{0,2},{1,3},{2,0},{3,1},{4,6},{5,7},{6,4},{7,5},{8,10},{9,11},{10,... | collective-permute-start | bytes 147464 | tf_op jit(solution)/shard_map/ppermute | solution.py:26
  41.0 3.9 %collective-permute-start.2 = (bf16[1,32,768]{2,1,0:T(8,128)(2,1)S(1)}, bf16[1,32,768]{2,1,0:T(8,128)(2,1)S(1)}, u32[]{:S(2)}, u32[]{:S(2)}) collective-permute-start(bf16[1,32,768]{2,1,0:T(8,128)(2,1)S(1)} %copy-done.15), channel_id=1, source_target_pairs={{0,3},{1,2},{2,1},{3,0},{4,7},{5,6},{6,5},{7,4},{8,11},{9,10},{10,... | collective-permute-start | bytes 147464 | tf_op jit(solution)/shard_map/ppermute | solution.py:26
  44.9 4.1 %collective-permute-start.3 = (bf16[1,32,768]{2,1,0:T(8,128)(2,1)S(1)}, bf16[1,32,768]{2,1,0:T(8,128)(2,1)S(1)}, u32[]{:S(2)}, u32[]{:S(2)}) collective-permute-start(bf16[1,32,768]{2,1,0:T(8,128)(2,1)S(1)} %copy-done.14), channel_id=1, source_target_pairs={{0,4},{1,5},{2,6},{3,7},{4,0},{5,1},{6,2},{7,3},{8,12},{9,13},{10,... | collective-permute-start | bytes 147464 | tf_op jit(solution)/shard_map/ppermute | solution.py:26
  49.0 3.5 %collective-permute-start.4 = (bf16[1,32,768]{2,1,0:T(8,128)(2,1)S(1)}, bf16[1,32,768]{2,1,0:T(8,128)(2,1)S(1)}, u32[]{:S(2)}, u32[]{:S(2)}) collective-permute-start(bf16[1,32,768]{2,1,0:T(8,128)(2,1)S(1)} %copy-done.13), channel_id=1, source_target_pairs={{0,5},{1,4},{2,7},{3,6},{4,1},{5,0},{6,3},{7,2},{8,13},{9,12},{10,... | collective-permute-start | bytes 147464 | tf_op jit(solution)/shard_map/ppermute | solution.py:26
  52.6 5.0 %collective-permute-start.5 = (bf16[1,32,768]{2,1,0:T(8,128)(2,1)S(1)}, bf16[1,32,768]{2,1,0:T(8,128)(2,1)S(1)}, u32[]{:S(2)}, u32[]{:S(2)}) collective-permute-start(bf16[1,32,768]{2,1,0:T(8,128)(2,1)S(1)} %copy-done.12), channel_id=1, source_target_pairs={{0,6},{1,7},{2,4},{3,5},{4,2},{5,3},{6,0},{7,1},{8,14},{9,15},{10,... | collective-permute-start | bytes 147464 | tf_op jit(solution)/shard_map/ppermute | solution.py:26
  57.6 4.4 %collective-permute-start.6 = (bf16[1,32,768]{2,1,0:T(8,128)(2,1)S(1)}, bf16[1,32,768]{2,1,0:T(8,128)(2,1)S(1)}, u32[]{:S(2)}, u32[]{:S(2)}) collective-permute-start(bf16[1,32,768]{2,1,0:T(8,128)(2,1)S(1)} %copy-done.11), channel_id=1, source_target_pairs={{0,7},{1,6},{2,5},{3,4},{4,3},{5,2},{6,1},{7,0},{8,15},{9,14},{10,... | collective-permute-start | bytes 147464 | tf_op jit(solution)/shard_map/ppermute | solution.py:26
  62.0 5.0 %collective-permute-start.7 = (bf16[1,32,768]{2,1,0:T(8,128)(2,1)S(1)}, bf16[1,32,768]{2,1,0:T(8,128)(2,1)S(1)}, u32[]{:S(2)}, u32[]{:S(2)}) collective-permute-start(bf16[1,32,768]{2,1,0:T(8,128)(2,1)S(1)} %copy-done.10), channel_id=1, source_target_pairs={{0,8},{1,9},{2,10},{3,11},{4,12},{5,13},{6,14},{7,15},{8,0},{9,1},... | collective-permute-start | bytes 147464 | tf_op jit(solution)/shard_map/ppermute | solution.py:26
  67.0 4.6 %collective-permute-start.8 = (bf16[1,32,768]{2,1,0:T(8,128)(2,1)S(1)}, bf16[1,32,768]{2,1,0:T(8,128)(2,1)S(1)}, u32[]{:S(2)}, u32[]{:S(2)}) collective-permute-start(bf16[1,32,768]{2,1,0:T(8,128)(2,1)S(1)} %copy-done.9), channel_id=1, source_target_pairs={{0,9},{1,8},{2,11},{3,10},{4,13},{5,12},{6,15},{7,14},{8,1},{9,0},... | collective-permute-start | bytes 147464 | tf_op jit(solution)/shard_map/ppermute | solution.py:26
  71.6 7.2 %collective-permute-start.9 = (bf16[1,32,768]{2,1,0:T(8,128)(2,1)S(1)}, bf16[1,32,768]{2,1,0:T(8,128)(2,1)S(1)}, u32[]{:S(2)}, u32[]{:S(2)}) collective-permute-start(bf16[1,32,768]{2,1,0:T(8,128)(2,1)S(1)} %copy-done.8), channel_id=1, source_target_pairs={{0,10},{1,11},{2,8},{3,9},{4,14},{5,15},{6,12},{7,13},{8,2},{9,3},... | collective-permute-start | bytes 147464 | tf_op jit(solution)/shard_map/ppermute | solution.py:26
  74.2 37.8 %all-to-all-start = ((bf16[16,2,12288]{2,1,0:T(2,128)(2,1)}), bf16[16,2,12288]{2,1,0:T(2,128)(2,1)S(1)}, u32[]{:S(2)}, u32[]{:S(2)}) async-start(bf16[16,2,12288]{2,1,0:T(2,128)(2,1)} %reshape.123), calls=%async_computation | async-start | bytes 1572864 | tf_op jit(solution)/shard_map/all_to_all | solution.py:51
  78.8 23.1 %collective-permute-start.10 = (bf16[1,32,768]{2,1,0:T(8,128)(2,1)S(1)}, bf16[1,32,768]{2,1,0:T(8,128)(2,1)S(1)}, u32[]{:S(2)}, u32[]{:S(2)}) collective-permute-start(bf16[1,32,768]{2,1,0:T(8,128)(2,1)S(1)} %get-tuple-element.38), channel_id=1, source_target_pairs={{0,11},{1,10},{2,9},{3,8},{4,15},{5,14},{6,13},{7,12},{8,3},{9,2},... | collective-permute-start | bytes 147464 | tf_op jit(solution)/shard_map/ppermute | solution.py:26
  119.3 4.8 %copy-start.4 = (bf16[16,32,768]{2,0,1:T(8,128)(2,1)S(1)}, bf16[16,32,768]{2,0,1:T(8,128)(2,1)}, u32[]{:S(2)}) copy-start(bf16[16,32,768]{2,0,1:T(8,128)(2,1)} %get-tuple-element.32) | copy-start | bytes 2359300
  120.4 22.3 %all-to-all-start.3 = ((bf16[16,32,768]{2,1,0:T(8,128)(2,1)}), bf16[16,32,768]{2,1,0:T(8,128)(2,1)S(1)}, u32[]{:S(2)}, u32[]{:S(2)}) async-start(bf16[16,32,768]{2,1,0:T(8,128)(2,1)} %copy.49), calls=%async_computation.3 | async-start | bytes 1572864 | tf_op jit(solution)/shard_map/all_to_all | solution.py:78
  142.7 24.1 %all-to-all-start.2 = ((bf16[16,32,768]{2,1,0:T(8,128)(2,1)}), bf16[16,32,768]{2,1,0:T(8,128)(2,1)S(1)}, u32[]{:S(2)}, u32[]{:S(2)}) async-start(bf16[16,32,768]{2,1,0:T(8,128)(2,1)} %copy.45), calls=%async_computation.2 | async-start | bytes 1572864 | tf_op jit(solution)/shard_map/all_to_all | solution.py:79
  166.8 50.0 %all-to-all-start.4 = ((bf16[16,32,768]{2,1,0:T(8,128)(2,1)}), bf16[16,32,768]{2,1,0:T(8,128)(2,1)S(1)}, u32[]{:S(2)}, u32[]{:S(2)}) async-start(bf16[16,32,768]{2,1,0:T(8,128)(2,1)} %copy.50), calls=%async_computation.4 | async-start | bytes 1572864 | tf_op jit(solution)/shard_map/all_to_all | solution.py:80
  (7 other events, 11.0 us)
